TPU v7x, 32 devices: a whole 2x2x4 slice. The times are simulated.
32 devices in a mesh: row: 8 (over y, x, core), src: 4 (over z).
Axes of the slice: x: 2, y: 2, z: 4, core: 2. Of those that a mesh axis runs over, the one named last changes fastest.
Arguments:
- traces: bfloat16 [16384, 128, 512], P('row', 'src'), may hold values from -6 to 6
- row_source: int32 [16384], P('row'), may hold values from 0 to 16383, as said below
- slice_data: bfloat16 [2, 16384, 8, 2048], P(None, 'row', None, 'src'), may hold values from -0.03125 to 0.03125
- wavelet_inverse: float32 [2], replicated, may hold values from 0.3 to 0.8
Outputs:
- multiples: float32 [16384, 2, 128], P(('row', 'src'))
- primaries: float32 [16384, 2, 128], P(('row', 'src'))
Inputs may be any that keep to these rules, and one draw needn't show every extreme that they name: `row_source`: every recording row is named exactly once; entry e * 2048 + p names a recording row whose index modulo 2048 lies in [e * 256, (e + 1) * 256).
All inputs are finite; a program needn't handle non-finite values.
Results may differ from a plain program's by a relative error of at most 0.0056.
Values may be sent and summed in bfloat16 or wider, within the bound.
No kernel may reach another device: no remote copies, remote signals or barrier semaphores. Data moves between devices by JAX's collectives and lax.ppermute only.
A program may use at most 192 MiB of HBM per device.

v0:
```python
import jax
import jax.numpy as jnp
from jax import lax
from jax.sharding import PartitionSpec as P

FREQ = 61
ITERS = 3


def dft_kernel(samples):
    ticks = jnp.arange(samples, dtype=jnp.int32)
    moment = ticks.astype(jnp.float32)
    ramp_len = samples // 8
    rising = 0.5 - 0.5 * jnp.cos(jnp.pi * (moment + 0.5) / ramp_len)
    falling = 0.5 - 0.5 * jnp.cos(jnp.pi * (samples - moment - 0.5) / ramp_len)
    taper = jnp.where(
        ticks < ramp_len,
        rising,
        jnp.where(ticks >= samples - ramp_len, falling, jnp.ones_like(rising)),
    )
    wrapped = ticks * FREQ % samples
    angles = 2.0 * jnp.pi / samples * wrapped.astype(jnp.float32)
    factor = 1.0 / jnp.sqrt(jnp.float32(samples))
    table = jnp.stack([taper * jnp.cos(angles) * factor, -taper * jnp.sin(angles) * factor], axis=1)
    return table.astype(jnp.bfloat16)


def combine_parts(real_terms, imag_terms, shot_count):
    pred_real = real_terms[:, :shot_count] - imag_terms[:, shot_count:]
    pred_imag = real_terms[:, shot_count:] + imag_terms[:, :shot_count]
    return jnp.stack([pred_real, pred_imag], axis=1)


def body(traces, row_source, slice_data, wavelet_inverse):
    block_rows, shot_local, samples = traces.shape
    kernel = dft_kernel(samples)
    spectra = jnp.dot(
        traces.reshape(block_rows * shot_local, samples), kernel, preferred_element_type=jnp.float32
    )
    spectra = jnp.transpose(spectra.reshape(block_rows, shot_local, 2), (0, 2, 1)).astype(
        jnp.bfloat16
    )
    arrived = lax.all_to_all(spectra, "row", split_axis=0, concat_axis=0, tiled=True)
    group_rows = block_rows // lax.axis_size("row")
    located = row_source // block_rows * group_rows + row_source % group_rows
    ordered = arrived[located]
    slice_rows = block_rows // lax.axis_size("src")
    panel = lax.all_to_all(ordered, "src", split_axis=0, concat_axis=2, tiled=True)
    shot_count = panel.shape[2]
    base = panel.astype(jnp.float32)
    wave_real = wavelet_inverse[0]
    wave_imag = wavelet_inverse[1]
    real_data = slice_data[0].reshape(block_rows, -1)
    imag_data = slice_data[1].reshape(block_rows, -1)
    estimate = panel
    predicted = jnp.zeros((slice_rows, 2, shot_count), jnp.float32)
    primaries = base
    for iteration in range(ITERS):
        gathered = lax.all_gather(estimate, "row", axis=0, tiled=True)
        stacked_all = gathered.reshape(gathered.shape[0], 2 * shot_count)
        real_terms = jnp.dot(real_data, stacked_all, preferred_element_type=jnp.float32)
        imag_terms = jnp.dot(imag_data, stacked_all, preferred_element_type=jnp.float32)
        predicted = lax.psum_scatter(
            combine_parts(real_terms, imag_terms, shot_count),
            "src",
            scatter_dimension=0,
            tiled=True,
        )
        next_real = base[:, 0] - (wave_real * predicted[:, 0] - wave_imag * predicted[:, 1])
        next_imag = base[:, 1] - (wave_real * predicted[:, 1] + wave_imag * predicted[:, 0])
        primaries = jnp.stack([next_real, next_imag], axis=1)
        estimate = primaries.astype(jnp.bfloat16)
    return (predicted, primaries)


def solution(mesh):
    in_specs = (P("row", "src", None), P("row"), P(None, "row", None, "src"), P())
    out_specs = (P(("row", "src"), None, None), P(("row", "src"), None, None))
    return jax.shard_map(body, mesh=mesh, in_specs=in_specs, out_specs=out_specs, check_vma=False)
```

profile of v0, /device:TPU:0, one launch (start us, length us, event | category | flops | bytes accessed | tf_op | source)
XLA Modules:
  0.0 388.9 jit_solution(9995842372074151427)
XLA Ops:
  7.2 0.1 multiply_convert_fusion
  7.3 25.4 %fusion = bf16[65536,2]{0,1:T(2,128)(2,1)S(1)} fusion(bf16[65536,512]{1,0:T(8,128)(2,1)} %bitcast, bf16[512,1]{0,1:T(2,128)(2,1)S(1)} %get-tuple-element.24, bf16[512,1]{0,1:T(2,128)(2,1)S(1)} %get-tuple-element.25), kind=kOutput, calls=%fused_computation.2 | convolution fusion | flops 134352896 | bytes 67373056 | tf_op jit(solution)/shard_map/dot_general | solution.py:37
  32.7 0.5 convert_element_type.54
  33.2 8.7 %copy.20 = bf16[2048,32,2]{1,2,0:T(2,128)(2,1)S(1)} copy(bf16[2048,32,2]{1,0,2:T(8,128)(2,1)S(1)} %convert_element_type.54) | data formatting | bytes 524288 | tf_op jit(solution)/shard_map/convert_element_type | solution.py:40
  41.9 1.7 reshape.153
  43.5 5.2 %all-to-all-start = ((bf16[8,2,8192]{2,1,0:T(2,128)(2,1)}), bf16[8,2,8192]{2,1,0:T(2,128)(2,1)S(1)}, u32[]{:S(2)}, u32[]{:S(2)}) async-start(bf16[8,2,8192]{2,1,0:T(2,128)(2,1)} %reshape.153), calls=%async_computation | async-start | bytes 524288 | tf_op jit(solution)/shard_map/all_to_all | solution.py:43
  48.8 6.9 %all-to-all-done = bf16[8,2,8192]{2,1,0:T(2,128)(2,1)S(1)} async-done(((bf16[8,2,8192]{2,1,0:T(2,128)(2,1)}), bf16[8,2,8192]{2,1,0:T(2,128)(2,1)S(1)}, u32[]{:S(2)}, u32[]{:S(2)}) %all-to-all-start) | async-done | bytes 262176 | tf_op jit(solution)/shard_map/all_to_all | solution.py:43
  55.6 0.5 reshape.154
  56.1 7.1 %gather_fusion = bf16[2048,2,32]{2,1,0:T(2,128)(2,1)S(1)} fusion(bf16[2048,2,32]{2,1,0:T(2,128)(2,1)S(1)} %reshape.154, s32[2048]{0:T(1024)S(1)} %fusion.10), kind=kCustom, calls=%fused_computation | custom fusion | bytes 532480 | tf_op jit(solution)/shard_map/gather | solution.py:46
  63.2 1.0 reshape.155
  64.2 12.9 %all_to_all.23 = bf16[4,2,16384]{2,1,0:T(2,128)(2,1)S(1)} all-to-all(bf16[4,2,16384]{2,1,0:T(2,128)(2,1)S(1)} %reshape.155), channel_id=1, replica_groups=mesh['row'=8,'src'=4] {'src'}, dimensions={0} | all-to-all | bytes 524288 | tf_op jit(solution)/shard_map/all_to_all | solution.py:48
  77.0 0.5 reshape.156
  77.5 1.8 copy.14
  79.3 0.2 reduce-scatter.4.cloned.1.call-start
  79.6 12.1 %fusion.30 = (bf16[1,2048,8,512]{3,2,1,0:T(8,128)(2,1)S(1)}, bf16[1,2048,8,512]{3,2,1,0:T(8,128)(2,1)S(1)}) fusion(bf16[2,2048,8,512]{3,2,1,0:T(8,128)(2,1)} %param.6), kind=kLoop, calls=%fused_computation.75 | loop fusion | bytes 67108864 | tf_op jit(solution)/shard_map/slice | solution.py:53
  91.7 10.6 %copy.17 = bf16[256,8,8,512]{3,1,2,0:T(8,128)(2,1)} copy(bf16[256,8,8,512]{3,2,1,0:T(8,128)(2,1)S(1)} %bitcast.62) | data formatting | bytes 33554432
  102.3 10.6 %copy.18 = bf16[256,8,8,512]{3,1,2,0:T(8,128)(2,1)} copy(bf16[256,8,8,512]{3,2,1,0:T(8,128)(2,1)S(1)} %bitcast.61) | data formatting | bytes 33554432
  112.9 8.7 %convolution_bitcast_fusion.4 = f32[2048,256]{0,1:T(8,128)S(1)} fusion(bf16[4096,256]{0,1:T(8,128)(2,1)} %bitcast.72, bf16[2048,4096]{1,0:T(8,128)(2,1)} %bitcast.66), kind=kOutput, calls=%fused_computation.7 | convolution fusion | flops 4294967296 | bytes 20971520 | tf_op jit(solution)/shard_map/dot_general | solution.py:62
  121.6 12.3 %convolution_bitcast_fusion.5 = f32[2048,256]{0,1:T(8,128)} fusion(bf16[4096,256]{0,1:T(8,128)(2,1)} %bitcast.73, bf16[2048,4096]{1,0:T(8,128)(2,1)} %bitcast.63), kind=kOutput, calls=%fused_computation.8 | convolution fusion | flops 4294967296 | bytes 20971520 | tf_op jit(solution)/shard_map/dot_general | solution.py:61
  133.9 1.8 fusion.6
  135.7 1.5 pad_maximum_fusion
  137.2 0.0 all-gather.6.cloned.1.call-start
  137.2 0.6 copy-done.3
  137.8 0.6 fusion.31
  138.4 0.1 bitcast_convert_fusion
  138.5 40.7 %reduce-scatter.4.cloned.1.call-done = f32[512,2,128]{0,2,1:T(8,128)} async-done(((f32[2048,2,128]{0,2,1:T(8,128)}), f32[512,2,128]{0,2,1:T(8,128)}) %reduce-scatter.4.cloned.1.call-update) | async-done | bytes 524304 | tf_op jit(solution)/shard_map/reduce_scatter | solution.py:63
  179.2 2.4 subtract_convert_fusion.3
  181.6 0.7 pad_maximum_fusion.4
  182.4 0.3 reduce-scatter.6.cloned.1.call-start
  182.6 27.4 %all-gather.6.cloned.1.call-done = bf16[4096,2,128]{0,2,1:T(8,128)(2,1)} async-done(((bf16[512,2,128]{0,2,1:T(8,128)(2,1)}), bf16[4096,2,128]{0,2,1:T(8,128)(2,1)}) %all-gather.6.cloned.1.call-update) | async-done | bytes 2097168 | tf_op jit(solution)/shard_map/all_gather | solution.py:59
  210.0 8.7 %convolution_bitcast_fusion.2 = f32[2048,256]{0,1:T(8,128)S(1)} fusion(bf16[4096,256]{0,1:T(8,128)(2,1)} %bitcast.76, bf16[2048,4096]{1,0:T(8,128)(2,1)} %bitcast.67), kind=kOutput, calls=%fused_computation.5 | convolution fusion | flops 4294967296 | bytes 20971520 | tf_op jit(solution)/shard_map/dot_general | solution.py:62
  218.8 12.3 %convolution_bitcast_fusion.3 = f32[2048,256]{0,1:T(8,128)} fusion(bf16[4096,256]{0,1:T(8,128)(2,1)} %bitcast.77, bf16[2048,4096]{1,0:T(8,128)(2,1)} %bitcast.64), kind=kOutput, calls=%fused_computation.6 | convolution fusion | flops 4294967296 | bytes 20971520 | tf_op jit(solution)/shard_map/dot_general | solution.py:61
  231.1 1.8 fusion.4
  232.9 1.5 pad_maximum_fusion.1
  234.4 0.0 all-gather.8.cloned.1.call-start
  234.4 44.0 %reduce-scatter.6.cloned.1.call-done = f32[512,2,128]{0,2,1:T(8,128)} async-done(((f32[2048,2,128]{0,2,1:T(8,128)}), f32[512,2,128]{0,2,1:T(8,128)}) %reduce-scatter.6.cloned.1.call-update) | async-done | bytes 524304 | tf_op jit(solution)/shard_map/reduce_scatter | solution.py:63
  278.4 2.4 subtract_convert_fusion.1
  280.8 0.7 pad_maximum_fusion.5
  281.6 0.3 reduce-scatter.8.cloned.1.call-start
  281.9 27.4 %all-gather.8.cloned.1.call-done = bf16[4096,2,128]{0,2,1:T(8,128)(2,1)} async-done(((bf16[512,2,128]{0,2,1:T(8,128)(2,1)}), bf16[4096,2,128]{0,2,1:T(8,128)(2,1)}) %all-gather.8.cloned.1.call-update) | async-done | bytes 2097168 | tf_op jit(solution)/shard_map/all_gather | solution.py:59
  309.2 8.7 %convolution_bitcast_fusion = f32[2048,256]{0,1:T(8,128)S(1)} fusion(bf16[4096,256]{0,1:T(8,128)(2,1)} %bitcast.74, bf16[2048,4096]{1,0:T(8,128)(2,1)} %bitcast.68), kind=kOutput, calls=%fused_computation.3 | convolution fusion | flops 4294967296 | bytes 20971520 | tf_op jit(solution)/shard_map/dot_general | solution.py:62
  318.0 12.3 %convolution_bitcast_fusion.1 = f32[2048,256]{0,1:T(8,128)} fusion(bf16[4096,256]{0,1:T(8,128)(2,1)} %bitcast.75, bf16[2048,4096]{1,0:T(8,128)(2,1)} %bitcast.65), kind=kOutput, calls=%fused_computation.4 | convolution fusion | flops 4294967296 | bytes 20971520 | tf_op jit(solution)/shard_map/dot_general | solution.py:61
  330.3 1.8 fusion.2
  332.1 1.5 pad_maximum_fusion.2
  333.6 44.0 %reduce-scatter.8.cloned.1.call-done = f32[512,2,128]{0,2,1:T(8,128)} async-done(((f32[2048,2,128]{0,2,1:T(8,128)}), f32[512,2,128]{0,2,1:T(8,128)}) %reduce-scatter.8.cloned.1.call-update) | async-done | bytes 524304 | tf_op jit(solution)/shard_map/reduce_scatter | solution.py:63
  377.6 2.5 subtract_subtract_fusion
  380.1 1.0 copy.16
  381.1 1.0 copy.15
  (17 shorter events, 0.2 us)
Async XLA Ops:
  33.2 15.6 %copy-start.2 = (s32[2048]{0:T(1024)S(1)}, s32[2048]{0:T(1024)}, u32[]{:S(2)}) copy-start(s32[2048]{0:T(1024)} %param.5) | copy-start | bytes 24580
  43.5 12.1 %all-to-all-start = ((bf16[8,2,8192]{2,1,0:T(2,128)(2,1)}), bf16[8,2,8192]{2,1,0:T(2,128)(2,1)S(1)}, u32[]{:S(2)}, u32[]{:S(2)}) async-start(bf16[8,2,8192]{2,1,0:T(2,128)(2,1)} %reshape.153), calls=%async_computation | async-start | bytes 524288 | tf_op jit(solution)/shard_map/all_to_all | solution.py:43
  48.7 64.2 %all-gather.4.cloned.1.call-start = ((), (), s32[]{:S(2)}) async-start(), calls=%async_computation.5 | async-start | bytes 2359296 | tf_op jit(solution)/shard_map/all_gather | solution.py:59
  79.3 99.8 %reduce-scatter.4.cloned.1.call-start = ((), (), s32[]{:S(2)}) async-start(), calls=%async_computation.6 | async-start | bytes 2621440 | tf_op jit(solution)/shard_map/reduce_scatter | solution.py:63
  137.2 0.7 copy-start.3
  137.2 1.3 copy-start
  137.2 72.8 %all-gather.6.cloned.1.call-start = ((), (), s32[]{:S(2)}) async-start(), calls=%async_computation.7 | async-start | bytes 2359296 | tf_op jit(solution)/shard_map/all_gather | solution.py:59
  182.4 96.0 %reduce-scatter.6.cloned.1.call-start = ((), (), s32[]{:S(2)}) async-start(), calls=%async_computation.8 | async-start | bytes 2621440 | tf_op jit(solution)/shard_map/reduce_scatter | solution.py:63
  234.4 74.9 %all-gather.8.cloned.1.call-start = ((), (), s32[]{:S(2)}) async-start(), calls=%async_computation.9 | async-start | bytes 2359296 | tf_op jit(solution)/shard_map/all_gather | solution.py:59
  281.6 96.0 %reduce-scatter.8.cloned.1.call-start = ((), (), s32[]{:S(2)}) async-start(), calls=%async_computation.10 | async-start | bytes 2621440 | tf_op jit(solution)/shard_map/reduce_scatter | solution.py:63
  377.6 3.5 copy-start.1
Sparse Core Ops, SparseCore 0:
  79.5 26.1 all-gather.3
  137.3 41.8 reduce-scatter.3
  182.5 27.5 all-gather.5
  234.5 43.8 reduce-scatter.5
  281.7 27.5 all-gather.7
  333.7 43.8 reduce-scatter.7
where the time goes:
time: 390 us; the launch traced here: 389 us
  waiting for transfers between devices  190 us (49%)
  matrix products  88.5 us (23%)
  local copies, waits for them, and re-layouts  58.1 us (15%)
  other arithmetic  18.7 us (5%)
  between operations  14.3 us (4%)
  blocking collectives  12.9 us (3%)
  starting transfers between devices  6.08 us (2%)
    reduce_scatter x3, waiting for transfers between devices, body(): lax.psum_scatter(combine_parts(real_terms, imag_terms, shot_count), 'src'...  129 us
    all_gather x3, waiting for transfers between devices, body(): gathered = lax.all_gather(estimate, 'row', axis=0, tiled=True)  54.8 us
    dot_general x3, matrix products, body(): jnp.dot(real_data, stacked_all, preferred_element_type=jnp.float32)  36.9 us
    unnamed x16, local copies, waits for them, and re-layouts  27.4 us
    dot_general x3, matrix products, body(): jnp.dot(imag_data, stacked_all, preferred_element_type=jnp.float32)  26.2 us
    dot_general x1, matrix products, body(): jnp.dot(traces.reshape(block_rows * shot_local, samples), kernel, preferr...  25.4 us
    all_to_all x1, blocking collectives, body(): lax.all_to_all(ordered, 'src', split_axis=0, concat_axis=2, tiled=True)  12.9 us
    slice x1, local copies, waits for them, and re-layouts, body(): real_data = slice_data[0].reshape(block_rows, -1)  12.1 us
  transfers between devices with their start and end apart: 7, of which 6 were waited for; matrix products, arithmetic and copies ran while one was open for 9% of the time, Pallas kernels for 0%

commit v1 on v0

v1 whole, which is shorter than its diff:
```python
import functools

import jax
import jax.numpy as jnp
import ml_dtypes
import numpy as np
from jax import lax
from jax.experimental import pallas as pl
from jax.experimental.pallas import tpu as pltpu
from jax.sharding import PartitionSpec as P

FREQ = 61
ITERS = 3
LANES = 128
VMEM = pl.BlockSpec(memory_space=pltpu.VMEM)
SMEM = pl.BlockSpec(memory_space=pltpu.SMEM)


def dft_table(samples):
    ticks = np.arange(samples, dtype=np.int32)
    moment = ticks.astype(np.float32)
    ramp_len = samples // 8
    pi = np.float32(np.pi)
    half = np.float32(0.5)
    rising = half - half * np.cos(pi * (moment + half) / np.float32(ramp_len))
    falling = half - half * np.cos(pi * (np.float32(samples) - moment - half) / np.float32(ramp_len))
    taper = np.where(
        ticks < ramp_len, rising, np.where(ticks >= samples - ramp_len, falling, np.ones_like(rising))
    )
    wrapped = ticks * FREQ % samples
    angles = np.float32(2.0 * np.pi / samples) * wrapped.astype(np.float32)
    factor = np.float32(1.0) / np.sqrt(np.float32(samples))
    table = np.stack([taper * np.cos(angles) * factor, -taper * np.sin(angles) * factor], axis=1)
    return table.astype(ml_dtypes.bfloat16)


def params(megabytes):
    return pltpu.CompilerParams(vmem_limit_bytes=megabytes * 2**20)


def cost(flops, moved):
    return pl.CostEstimate(flops=int(flops), bytes_accessed=int(moved), transcendentals=0)


def spectra_kernel(packs, place_ref, traces_ref, table_ref, *out_refs):
    block, shots, samples = traces_ref.shape
    width = 2 * shots
    shot = lax.broadcasted_iota(jnp.int32, (1, shots, LANES), 1)
    lane = lax.broadcasted_iota(jnp.int32, (1, shots, LANES), 2)
    own = lane % shots == shot
    chunk = min(block, 16)
    rows = []
    for start in range(0, block, chunk):
        part = traces_ref[start : start + chunk].reshape(chunk * shots, samples)
        terms = jnp.dot(part, table_ref[...], preferred_element_type=jnp.float32)
        rows.append(jnp.sum(jnp.where(own, terms.reshape(chunk, shots, LANES), 0.0), axis=1))
    spectra = jnp.concatenate(rows, axis=0)
    short = block // packs
    column = lax.broadcasted_iota(jnp.int32, (short, LANES), 1)
    packed = spectra[:short]
    for part in range(1, packs):
        packed = jnp.where(column // width == part, spectra[part * short : (part + 1) * short], packed)
    packed = packed.astype(jnp.bfloat16)
    steps = pl.num_programs(0) // len(out_refs)
    for turn, out_ref in enumerate(out_refs):

        @pl.when(pl.program_id(0) // steps == turn)
        def _():
            out_ref[0] = packed


def make_spectra(traces, place, n_row, packs, block):
    block_rows, shots, samples = traces.shape
    steps = block_rows // n_row // block
    short = block // packs
    table = jnp.asarray(np.tile(np.repeat(dft_table(samples), shots, axis=1), (1, packs)))

    def source(step, place_ref):
        return (place_ref[0] ^ (step // steps)) * steps + step % steps, 0, 0

    def target(turn, step, place_ref):
        return jnp.clip(step - turn * steps, 0, steps - 1), 0, 0

    outs = pl.pallas_call(
        functools.partial(spectra_kernel, packs),
        grid_spec=pltpu.PrefetchScalarGridSpec(
            num_scalar_prefetch=1,
            grid=(n_row * steps,),
            in_specs=[
                pl.BlockSpec((block, shots, samples), source),
                pl.BlockSpec((samples, LANES), lambda step, place_ref: (0, 0)),
            ],
            out_specs=[
                pl.BlockSpec((1, short, LANES), functools.partial(target, turn)) for turn in range(n_row)
            ],
        ),
        out_shape=[jax.ShapeDtypeStruct((steps, short, LANES), jnp.bfloat16)] * n_row,
        compiler_params=params(48),
        cost_estimate=cost(2 * traces.size * LANES, 2 * traces.size),
        name="spectra",
    )(place, traces, table)
    return [out.reshape(steps * short, LANES) for out in outs]


def order_kernel(packs, n_src, place_ref, code_ref, *refs):
    pieces, out_refs = refs[:-n_src], refs[-n_src:]
    width = LANES // packs
    held = jnp.concatenate([ref[...] for ref in pieces], axis=0)
    rolled = [held] + [
        pltpu.roll(held.astype(jnp.float32), turn * width, 1).astype(jnp.bfloat16) for turn in range(1, packs)
    ]
    table = jnp.concatenate(rolled, axis=1)
    depth = table.shape[0]
    slice_rows = code_ref.shape[0] // n_src
    short = slice_rows // packs
    column = lax.broadcasted_iota(jnp.int32, (short, LANES), 1)
    for turn, out_ref in enumerate(out_refs):
        first = pl.multiple_of((place_ref[1] ^ turn) * slice_rows, slice_rows)
        packed = None
        for part in range(packs):
            code = code_ref[pl.ds(pl.multiple_of(first + part * short, short), short), :]
            position, side = code // packs, code % packs
            hits = []
            for start in range(0, depth, LANES):
                hits.append(jnp.where(position == column + start, 1.0, 0.0).astype(jnp.bfloat16))
            chosen = jnp.concatenate(hits, axis=1)[:, :depth]
            rows = jnp.dot(chosen, table, preferred_element_type=jnp.float32)
            moved = rows[:, :LANES]
            for turned in range(1, packs):
                moved = jnp.where(
                    (part - side + packs) % packs == turned, rows[:, turned * LANES : (turned + 1) * LANES], moved
                )
            packed = moved if packed is None else jnp.where(column // width == part, moved, packed)
        out_ref[...] = packed.astype(jnp.bfloat16)


def make_order(code, pieces, place, n_src, packs):
    slice_rows = code.shape[0] // n_src
    return pl.pallas_call(
        functools.partial(order_kernel, packs, n_src),
        in_specs=[SMEM] + [VMEM] * (1 + len(pieces)),
        out_specs=[VMEM] * n_src,
        out_shape=[jax.ShapeDtypeStruct((slice_rows // packs, LANES), jnp.bfloat16)] * n_src,
        compiler_params=params(48),
        cost_estimate=cost(2 * code.shape[0] * len(pieces) * pieces[0].size * packs, 4 * code.size),
        name="order",
    )(place, code, *pieces)


def panel_kernel(packs, place_ref, *refs):
    pieces, panel_ref = refs[:-1], refs[-1]
    short = pieces[0].shape[0]
    width = LANES // packs
    shots = width // 2
    columns = panel_ref.shape[1]
    whole_shots = columns // 2
    lane = lax.broadcasted_iota(jnp.int32, (LANES, packs * columns), 0)
    target = lax.broadcasted_iota(jnp.int32, (LANES, packs * columns), 1)
    goes = lane // width * columns + lane % width // shots * whole_shots + lane % shots
    total = None
    for turn, piece in enumerate(pieces):
        shift = (place_ref[1] ^ turn) * shots
        chosen = jnp.where(target == goes + shift, 1.0, 0.0).astype(jnp.bfloat16)
        term = jnp.dot(piece[...], chosen, preferred_element_type=jnp.float32)
        total = term if total is None else total + term
    for part in range(packs):
        panel_ref[part * short : (part + 1) * short, :] = total[:, part * columns : (part + 1) * columns].astype(
            jnp.bfloat16
        )


def make_panel(pieces, place, packs):
    short = pieces[0].shape[0]
    columns = len(pieces) * (LANES // packs)
    return pl.pallas_call(
        functools.partial(panel_kernel, packs),
        in_specs=[SMEM] + [VMEM] * len(pieces),
        out_specs=VMEM,
        out_shape=jax.ShapeDtypeStruct((short * packs, columns), jnp.bfloat16),
        compiler_params=params(32),
        cost_estimate=cost(2 * len(pieces) * short * LANES * packs * columns, 4 * short * packs * columns),
        name="panel",
    )(place, *pieces)


def relay_kernel(data_ref, out_ref):
    blocks, offsets = data_ref.shape[2:]
    turned = jnp.swapaxes(data_ref[0], 0, 1)
    for block in range(blocks):
        out_ref[:, block * offsets : (block + 1) * offsets] = turned[block]


def relay(slice_data, part, step_rows):
    _, block_rows, blocks, offsets = slice_data.shape
    return pl.pallas_call(
        relay_kernel,
        grid=(block_rows // step_rows,),
        in_specs=[pl.BlockSpec((1, step_rows, blocks, offsets), lambda step: (part, step, 0, 0))],
        out_specs=pl.BlockSpec((step_rows, blocks * offsets), lambda step: (step, 0)),
        out_shape=jax.ShapeDtypeStruct((block_rows, blocks * offsets), jnp.bfloat16),
        compiler_params=params(32),
        cost_estimate=cost(0, 2 * slice_data.size),
        name="relay",
    )(slice_data)


def terms_kernel(turns, place_ref, real_ref, imag_ref, *refs):
    pieces = refs[: -1 - len(turns)]
    out_refs, held = refs[-1 - len(turns) : -1], refs[-1]
    offsets, columns = pieces[0].shape
    depth = held.shape[0] // 2
    shots = columns // 2

    @pl.when(pl.program_id(0) == 0)
    def _():
        for turn, piece in enumerate(pieces):
            first = pl.multiple_of((place_ref[0] ^ turn) * offsets, offsets)
            held[pl.ds(first, offsets), :] = piece[...]
            second = pl.multiple_of(first + depth, offsets)
            held[pl.ds(second, offsets), :shots] = -piece[:, shots:]
            held[pl.ds(second, offsets), shots:] = piece[:, :shots]

    total = jnp.dot(real_ref[...], held[:depth], preferred_element_type=jnp.float32)
    total += jnp.dot(imag_ref[...], held[depth:], preferred_element_type=jnp.float32)
    steps = pl.num_programs(0) // len(turns)
    for number, out_ref in enumerate(out_refs):

        @pl.when(pl.program_id(0) // steps == number)
        def _():
            out_ref[...] = total.astype(out_ref.dtype)


def make_terms(real_data, imag_data, pieces, place, turns, slice_rows):
    depth = real_data.shape[1]
    offsets, columns = pieces[0].shape
    tile = min(slice_rows, 128)
    steps = slice_rows // tile

    def source(step, place_ref):
        index = step // steps
        turn = turns[-1]
        for number in range(len(turns) - 1):
            turn = jnp.where(index == number, turns[number], turn)
        return (place_ref[1] ^ turn) * steps + step % steps, 0

    def target(number, step, place_ref):
        return jnp.clip(step - number * steps, 0, steps - 1), 0

    whole = pl.BlockSpec((offsets, columns), lambda step, place_ref: (0, 0))
    rows = len(turns) * slice_rows
    return pl.pallas_call(
        functools.partial(terms_kernel, turns),
        grid_spec=pltpu.PrefetchScalarGridSpec(
            num_scalar_prefetch=1,
            grid=(len(turns) * steps,),
            in_specs=[pl.BlockSpec((tile, depth), source)] * 2 + [whole] * len(pieces),
            out_specs=[
                pl.BlockSpec((tile, columns), functools.partial(target, number)) for number in range(len(turns))
            ],
            scratch_shapes=[pltpu.VMEM((2 * depth, columns), jnp.bfloat16)],
        ),
        out_shape=[
            jax.ShapeDtypeStruct((slice_rows, columns), jnp.bfloat16 if turn else jnp.float32) for turn in turns
        ],
        compiler_params=params(48),
        cost_estimate=cost(4 * rows * depth * columns, 4 * rows * depth),
        name="terms",
    )(place, real_data, imag_data, *pieces)


def update(wave_ref, own_ref, others, panel_ref):
    predicted = own_ref[...]
    for other in others:
        predicted += other[...].astype(jnp.float32)
    shots = predicted.shape[1] // 2
    base = panel_ref[...].astype(jnp.float32)
    real, imag = predicted[:, :shots], predicted[:, shots:]
    next_real = base[:, :shots] - (wave_ref[0] * real - wave_ref[1] * imag)
    next_imag = base[:, shots:] - (wave_ref[0] * imag + wave_ref[1] * real)
    return real, imag, next_real, next_imag


def estimate_kernel(wave_ref, own_ref, *refs):
    *others, panel_ref, out_ref = refs
    shots = out_ref.shape[1] // 2
    _, _, next_real, next_imag = update(wave_ref, own_ref, others, panel_ref)
    out_ref[:, :shots] = next_real.astype(jnp.bfloat16)
    out_ref[:, shots:] = next_imag.astype(jnp.bfloat16)


def last_kernel(wave_ref, own_ref, *refs):
    *others, panel_ref, multiples_ref, primaries_ref = refs
    real, imag, next_real, next_imag = update(wave_ref, own_ref, others, panel_ref)
    multiples_ref[:, 0, :] = real
    multiples_ref[:, 1, :] = imag
    primaries_ref[:, 0, :] = next_real
    primaries_ref[:, 1, :] = next_imag


def make_update(wavelet, own, others, panel, last):
    rows, columns = panel.shape
    if last:
        shape = [jax.ShapeDtypeStruct((rows, 2, columns // 2), jnp.float32)] * 2
    else:
        shape = jax.ShapeDtypeStruct((rows, columns), jnp.bfloat16)
    return pl.pallas_call(
        last_kernel if last else estimate_kernel,
        in_specs=[SMEM] + [VMEM] * (2 + len(others)),
        out_specs=[VMEM] * 2 if last else VMEM,
        out_shape=shape,
        compiler_params=params(32),
        cost_estimate=cost(16 * rows * columns, 16 * rows * columns),
        name="update",
    )(wavelet, own, *others, panel)


def swap(array, axis, bits):
    size = lax.axis_size(axis)
    return lax.ppermute(array, axis, [(index, index ^ bits) for index in range(size)])


def spread(array, axis):
    size = lax.axis_size(axis)
    pieces = {0: array}
    for turn in range(2, size, 2):
        pieces[turn] = swap(array, axis, turn)
    for turn in range(0, size, 2):
        pieces[turn + 1] = swap(pieces[turn], axis, 1)
    return [pieces[turn] for turn in range(size)]


def body(traces, row_source, slice_data, wavelet_inverse):
    block_rows, shots, _ = traces.shape
    n_row, n_src = lax.axis_size("row"), lax.axis_size("src")
    row, src = lax.axis_index("row"), lax.axis_index("src")
    place = jnp.stack([row, src]).astype(jnp.int32)
    packs = LANES // (2 * shots)
    group_rows = block_rows // n_row
    slice_rows = block_rows // n_src
    block = min(group_rows, 128)
    short = block // packs

    spectra = make_spectra(traces, place, n_row, packs, block)
    arrived = [spectra[0]] + [swap(spectra[turn], "row", turn) for turn in range(1, n_row)]

    inside = row_source % group_rows
    position = (row_source // block_rows ^ row) * (group_rows // packs) + inside // block * short + inside % short
    code = position * packs + inside % block // short
    code = jnp.broadcast_to(code[:, None], (block_rows, LANES))
    ordered = make_order(code, arrived, place, n_src, packs)
    located = [ordered[0]] + [swap(ordered[turn], "src", turn) for turn in range(1, n_src)]
    panel = make_panel(located, place, packs)

    step_rows = min(block_rows, 128)
    real_data = relay(slice_data, 0, step_rows)
    imag_data = relay(slice_data, 1, step_rows)

    half = n_src // 2
    far = tuple(range(half, n_src))
    near = tuple(range(half - 1, -1, -1))
    estimate = panel
    for iteration in range(ITERS):
        pieces = spread(estimate, "row")
        terms = dict(zip(far, make_terms(real_data, imag_data, pieces, place, far, slice_rows)))
        arriving = [swap(terms[turn], "src", turn) for turn in far]
        terms.update(zip(near, make_terms(real_data, imag_data, pieces, place, near, slice_rows)))
        arriving += [swap(terms[turn], "src", turn) for turn in near if turn]
        estimate = make_update(wavelet_inverse, terms[0], arriving, panel, iteration == ITERS - 1)
    return tuple(estimate)


def solution(mesh):
    in_specs = (P("row", "src", None), P("row"), P(None, "row", None, "src"), P())
    out_specs = (P(("row", "src"), None, None), P(("row", "src"), None, None))
    return jax.shard_map(body, mesh=mesh, in_specs=in_specs, out_specs=out_specs, check_vma=False)
```

time: 390 us -> 260 us (0.67)
  Pallas kernels: 0 us -> 134 us
  waiting for transfers between devices: 190 us -> 76.2 us
  matrix products: 88.5 us -> 0 us
  local copies, waits for them, and re-layouts: 58.1 us -> 12.8 us
  starting transfers between devices: 6.08 us -> 35.3 us
  other arithmetic: 18.7 us -> 0.11 us
  between operations: 14.3 us -> 0.85 us
  blocking collectives: 12.9 us -> 0 us
    pallas_call x0 -> x14, Pallas kernels: none -> 134 us  [the longest x6 69.1 us: make_terms(): pl.pallas_call(functools.partial(terms_kernel, turns), grid_spec=pltpu.Pr...]
    reduce_scatter x3 -> x0, waiting for transfers between devices: 129 us -> none  [body(): lax.psum_scatter(combine_parts(real_terms, imag_terms, shot_count), 'src'...]
    dot_general x7 -> x0, matrix products: 88.5 us -> none  [the longest x3 36.9 us: body(): jnp.dot(real_data, stacked_all, preferred_element_type=jnp.float32)]
    ppermute x0 -> x40, waiting for transfers between devices: none -> 76.2 us  [swap(): lax.ppermute(array, axis, [(index, index ^ bits) for index in range(size)])]
    all_gather x3 -> x0, waiting for transfers between devices: 54.8 us -> none  [body(): gathered = lax.all_gather(estimate, 'row', axis=0, tiled=True)]
    ppermute x0 -> x40, starting transfers between devices: none -> 35.3 us  [swap(): lax.ppermute(array, axis, [(index, index ^ bits) for index in range(size)])]
    another operation x12 -> x1, other arithmetic: 16.2 us -> 0.08 us  [body(): place = jnp.stack([row, src]).astype(jnp.int32)]
    unnamed x16 -> x10, local copies, waits for them, and re-layouts: 27.4 us -> 12.4 us
  transfers between devices with their start and end apart: 7 -> 40, of which waited for: 6 -> 21; matrix products, arithmetic and copies ran while one was open for 9% -> 0% of each run, Pallas kernels for 0% -> 23%
where the time goes in v1:
time: 260 us; the launch traced here: 259 us
  Pallas kernels  134 us (52%)
  waiting for transfers between devices  76.2 us (29%)
  starting transfers between devices  35.3 us (14%)
  local copies, waits for them, and re-layouts  12.8 us (5%)
    ppermute x40, waiting for transfers between devices, swap(): lax.ppermute(array, axis, [(index, index ^ bits) for index in range(size)])  76.2 us
    pallas_call x6, Pallas kernels, make_terms(): pl.pallas_call(functools.partial(terms_kernel, turns), grid_spec=pltpu.Pr...  69.1 us
    ppermute x40, starting transfers between devices, swap(): lax.ppermute(array, axis, [(index, index ^ bits) for index in range(size)])  35.3 us
    pallas_call x1, Pallas kernels, make_spectra(): pl.pallas_call(functools.partial(spectra_kernel, packs), grid_spec=pltpu....  31.1 us
    pallas_call x2, Pallas kernels, relay(): pl.pallas_call(relay_kernel, grid=(block_rows // step_rows,), in_specs=[p...  26.1 us
    unnamed x10, local copies, waits for them, and re-layouts  12.4 us
  transfers between devices with their start and end apart: 40, of which 21 were waited for; matrix products, arithmetic and copies ran while one was open for 0% of the time, Pallas kernels for 23%

profile of v1, /device:TPU:0, one launch (start us, length us, event | category | flops | bytes accessed | tf_op | source)
XLA Modules:
  0.0 258.7 jit_solution(12389711979219462766)
XLA Ops:
  1.6 31.1 %spectra.1 = (bf16[2,64,128]{2,1,0:T(8,128)(2,1)S(1)}, bf16[2,64,128]{2,1,0:T(8,128)(2,1)S(1)}, bf16[2,64,128]{2,1,0:T(8,128)(2,1)S(1)}, bf16[2,64,128]{2,1,0:T(...) custom-call(s32[2]{0:T(128)S(1)} %pad_add_fusion.place_ref, ...), custom_call_target="tpu_custom_call" | custom-call | flops 8589934592 | bytes 67108864 | tf_op jit(solution)/shard_map/spectra/pallas_call | solution.py:84
  33.2 2.6 collective-permute-start.1
  35.8 1.8 collective-permute-start.3
  37.6 2.6 %collective-permute-start.5 = (bf16[128,128]{1,0:T(8,128)(2,1)S(1)}, bf16[128,128]{1,0:T(8,128)(2,1)S(1)}, u32[]{:S(2)}, u32[]{:S(2)}) collective-permute-start(bf16[128,128]{1,0:T(8,128)(2,1)S(1)} %bitcast.12), channel_id=1, source_target_pairs={{0,24},{4,28},{8,16},{12,20},{16,8},{20,12},{24,0},{28,4},{1,25},{... | collective-permute-start | bytes 98312 | tf_op jit(solution)/shard_map/ppermute | solution.py:319
  41.1 1.4 collective-permute-done.5.refs_6_
  42.4 2.0 collective-permute-done.6.refs_7_
  44.8 2.8 %order.1 = (bf16[256,128]{1,0:T(8,128)(2,1)S(1)}, bf16[256,128]{1,0:T(8,128)(2,1)S(1)}, bf16[256,128]{1,0:T(8,128)(2,1)S(1)}, bf16[256,128]{1,0:T(8,128)(2,1)S(1)}) custom-call(s32[2]{0:T(128)S(1)} %pad_add_fusion.place_ref, s32[2048,128]{1,0:T(8,128)S(1)} %broadcast_in_dim.2.code_ref, bf16[128,128]{1,0:T(8,128)(2,1)S(1)} %bitcast.10, ...), custom_call_target="tpu_custom_call" | custom-call | flops 1073741824 | bytes 1048576 | tf_op jit(solution)/shard_map/order/pallas_call | solution.py:139
  47.6 1.6 collective-permute-start.7
  49.3 2.6 collective-permute-start.8
  52.1 4.7 %collective-permute-done.8.refs_2_ = bf16[256,128]{1,0:T(8,128)(2,1)S(1)} collective-permute-done((bf16[256,128]{1,0:T(8,128)(2,1)S(1)}, bf16[256,128]{1,0:T(8,128)(2,1)S(1)}, u32[]{:S(2)}, u32[]{:S(2)}) %collective-permute-start.8) | collective-permute-done | bytes 65568 | tf_op jit(solution)/shard_map/ppermute | solution.py:319
  56.8 1.2 collective-permute-done.9.refs_3_
  59.6 1.1 collective-permute-start.13
  60.7 1.9 collective-permute-start.15
  62.6 5.8 %collective-permute-done.11.refs_2_ = bf16[512,256]{1,0:T(8,128)(2,1)S(1)} collective-permute-done((bf16[512,256]{1,0:T(8,128)(2,1)S(1)}, bf16[512,256]{1,0:T(8,128)(2,1)S(1)}, u32[]{:S(2)}, u32[]{:S(2)}) %collective-permute-start.11) | collective-permute-done | bytes 262176 | tf_op jit(solution)/shard_map/ppermute | solution.py:319
  68.3 3.3 %collective-permute-done.13.refs_4_ = bf16[512,256]{1,0:T(8,128)(2,1)S(1)} collective-permute-done((bf16[512,256]{1,0:T(8,128)(2,1)S(1)}, bf16[512,256]{1,0:T(8,128)(2,1)S(1)}, u32[]{:S(2)}, u32[]{:S(2)}) %collective-permute-start.13) | collective-permute-done | bytes 262176 | tf_op jit(solution)/shard_map/ppermute | solution.py:319
  72.1 13.0 %relay.2.real_ref = bf16[2048,4096]{1,0:T(8,128)(2,1)S(1)} custom-call(bf16[2,2048,8,512]{3,2,1,0:T(8,128)(2,1)} %data_ref.3), custom_call_target="tpu_custom_call" | custom-call | bytes 33554432 | tf_op jit(solution)/shard_map/relay/pallas_call | solution.py:195
  85.2 5.8 %copy-done = bf16[2048,4096]{1,0:T(8,128)(2,1)} copy-done((bf16[2048,4096]{1,0:T(8,128)(2,1)}, bf16[2048,4096]{1,0:T(8,128)(2,1)S(1)}, u32[]{:S(2)}) %copy-start) | copy-done | bytes 16777240
  91.0 13.0 %relay.3.imag_ref = bf16[2048,4096]{1,0:T(8,128)(2,1)S(1)} custom-call(bf16[2,2048,8,512]{3,2,1,0:T(8,128)(2,1)} %data_ref.3), custom_call_target="tpu_custom_call" | custom-call | bytes 33554432 | tf_op jit(solution)/shard_map/relay/pallas_call | solution.py:195
  104.0 5.8 %copy-done.1 = bf16[2048,4096]{1,0:T(8,128)(2,1)} copy-done((bf16[2048,4096]{1,0:T(8,128)(2,1)}, bf16[2048,4096]{1,0:T(8,128)(2,1)S(1)}, u32[]{:S(2)}) %copy-start.1) | copy-done | bytes 16777240
  109.8 11.5 %terms.7 = (bf16[512,256]{1,0:T(8,128)(2,1)S(1)}, bf16[512,256]{1,0:T(8,128)(2,1)S(1)}) custom-call(s32[2]{0:T(128)S(1)} %pad_add_fusion.place_ref, bf16[2048,4096]{1,0:T(8,128)(2,1)} %copy-done, bf16[2048,4096]{1,0:T(8,128)(2,1)} %copy-done.1, bf16[512,256]{1,0:T(8,128)(2,1)S(1)} %panel.1.refs_0_.refs_3_, ...), custom_call_target="tpu_custom_call" | custom-call | flops 4294967296 | bytes 16777216 | tf_op jit(solution)/shard_map/terms/pallas_call | solution.py:251
  121.3 2.2 collective-permute-start.17
  123.5 1.5 collective-permute-start.18
  125.0 11.5 %terms.6 = (bf16[512,256]{1,0:T(8,128)(2,1)S(1)}, f32[512,256]{1,0:T(8,128)S(1)}) custom-call(s32[2]{0:T(128)S(1)} %pad_add_fusion.place_ref, bf16[2048,4096]{1,0:T(8,128)(2,1)} %copy-done, bf16[2048,4096]{1,0:T(8,128)(2,1)} %copy-done.1, bf16[512,256]{1,0:T(8,128)(2,1)S(1)} %panel.1.refs_0_.refs_3_, bf16[512,256]{1,0:T(8,128)(2,1)S(1)} %collective-permute-done.10.refs_1_, ...), custom_call_target="tpu_custom_call" | custom-call | flops 4294967296 | bytes 16777216 | tf_op jit(solution)/shard_map/terms/pallas_call | solution.py:251
  136.5 6.0 %collective-permute-done.17.refs_0_ = bf16[512,256]{1,0:T(8,128)(2,1)S(1)} collective-permute-done((bf16[512,256]{1,0:T(8,128)(2,1)S(1)}, bf16[512,256]{1,0:T(8,128)(2,1)S(1)}, u32[]{:S(2)}, u32[]{:S(2)}) %collective-permute-start.17) | collective-permute-done | bytes 262176 | tf_op jit(solution)/shard_map/ppermute | solution.py:319
  142.5 4.8 %collective-permute-done.19.refs_2_ = bf16[512,256]{1,0:T(8,128)(2,1)S(1)} collective-permute-done((bf16[512,256]{1,0:T(8,128)(2,1)S(1)}, bf16[512,256]{1,0:T(8,128)(2,1)S(1)}, u32[]{:S(2)}, u32[]{:S(2)}) %collective-permute-start.19) | collective-permute-done | bytes 262176 | tf_op jit(solution)/shard_map/ppermute | solution.py:319
  148.1 1.6 collective-permute-start.21
  150.2 1.5 collective-permute-start.25
  151.6 5.7 %collective-permute-done.21.refs_2_ = bf16[512,256]{1,0:T(8,128)(2,1)S(1)} collective-permute-done((bf16[512,256]{1,0:T(8,128)(2,1)S(1)}, bf16[512,256]{1,0:T(8,128)(2,1)S(1)}, u32[]{:S(2)}, u32[]{:S(2)}) %collective-permute-start.21) | collective-permute-done | bytes 262176 | tf_op jit(solution)/shard_map/ppermute | solution.py:319
  157.3 5.9 %collective-permute-done.23.refs_4_ = bf16[512,256]{1,0:T(8,128)(2,1)S(1)} collective-permute-done((bf16[512,256]{1,0:T(8,128)(2,1)S(1)}, bf16[512,256]{1,0:T(8,128)(2,1)S(1)}, u32[]{:S(2)}, u32[]{:S(2)}) %collective-permute-start.23) | collective-permute-done | bytes 262176 | tf_op jit(solution)/shard_map/ppermute | solution.py:319
  163.7 1.0 collective-permute-done.24.refs_5_
  165.1 11.5 %terms.9 = (bf16[512,256]{1,0:T(8,128)(2,1)S(1)}, bf16[512,256]{1,0:T(8,128)(2,1)S(1)}) custom-call(s32[2]{0:T(128)S(1)} %pad_add_fusion.place_ref, bf16[2048,4096]{1,0:T(8,128)(2,1)} %copy-done, bf16[2048,4096]{1,0:T(8,128)(2,1)} %copy-done.1, bf16[512,256]{1,0:T(8,128)(2,1)S(1)} %update.3.refs_0_, bf16[512,256]{1,0:T(8,128)(2,1)S(1)} %collective-permute-done.20.refs_1_, ...), custom_call_target="tpu_custom_call" | custom-call | flops 4294967296 | bytes 16777216 | tf_op jit(solution)/shard_map/terms/pallas_call | solution.py:251
  176.7 2.3 collective-permute-start.28
  179.0 11.7 %terms.8 = (bf16[512,256]{1,0:T(8,128)(2,1)S(1)}, f32[512,256]{1,0:T(8,128)S(1)}) custom-call(s32[2]{0:T(128)S(1)} %pad_add_fusion.place_ref, bf16[2048,4096]{1,0:T(8,128)(2,1)} %copy-done, bf16[2048,4096]{1,0:T(8,128)(2,1)} %copy-done.1, bf16[512,256]{1,0:T(8,128)(2,1)S(1)} %update.3.refs_0_, bf16[512,256]{1,0:T(8,128)(2,1)S(1)} %collective-permute-done.20.refs_1_, ...), custom_call_target="tpu_custom_call" | custom-call | flops 4294967296 | bytes 16777216 | tf_op jit(solution)/shard_map/terms/pallas_call | solution.py:251
  190.7 1.2 collective-permute-start.29
  191.9 4.8 %collective-permute-done.27.refs_0_ = bf16[512,256]{1,0:T(8,128)(2,1)S(1)} collective-permute-done((bf16[512,256]{1,0:T(8,128)(2,1)S(1)}, bf16[512,256]{1,0:T(8,128)(2,1)S(1)}, u32[]{:S(2)}, u32[]{:S(2)}) %collective-permute-start.27) | collective-permute-done | bytes 262176 | tf_op jit(solution)/shard_map/ppermute | solution.py:319
  196.7 5.5 %collective-permute-done.29.refs_2_ = bf16[512,256]{1,0:T(8,128)(2,1)S(1)} collective-permute-done((bf16[512,256]{1,0:T(8,128)(2,1)S(1)}, bf16[512,256]{1,0:T(8,128)(2,1)S(1)}, u32[]{:S(2)}, u32[]{:S(2)}) %collective-permute-start.29) | collective-permute-done | bytes 262176 | tf_op jit(solution)/shard_map/ppermute | solution.py:319
  203.5 1.4 collective-permute-start.33
  205.0 1.5 collective-permute-start.35
  206.5 5.7 %collective-permute-done.31.refs_2_ = bf16[512,256]{1,0:T(8,128)(2,1)S(1)} collective-permute-done((bf16[512,256]{1,0:T(8,128)(2,1)S(1)}, bf16[512,256]{1,0:T(8,128)(2,1)S(1)}, u32[]{:S(2)}, u32[]{:S(2)}) %collective-permute-start.31) | collective-permute-done | bytes 262176 | tf_op jit(solution)/shard_map/ppermute | solution.py:319
  212.2 4.9 %collective-permute-done.33.refs_4_ = bf16[512,256]{1,0:T(8,128)(2,1)S(1)} collective-permute-done((bf16[512,256]{1,0:T(8,128)(2,1)S(1)}, bf16[512,256]{1,0:T(8,128)(2,1)S(1)}, u32[]{:S(2)}, u32[]{:S(2)}) %collective-permute-start.33) | collective-permute-done | bytes 262176 | tf_op jit(solution)/shard_map/ppermute | solution.py:319
  217.6 1.0 collective-permute-done.34.refs_5_
  219.0 11.5 %terms.11 = (bf16[512,256]{1,0:T(8,128)(2,1)S(1)}, bf16[512,256]{1,0:T(8,128)(2,1)S(1)}) custom-call(s32[2]{0:T(128)S(1)} %pad_add_fusion.place_ref, bf16[2048,4096]{1,0:T(8,128)(2,1)} %copy-done, bf16[2048,4096]{1,0:T(8,128)(2,1)} %copy-done.1, bf16[512,256]{1,0:T(8,128)(2,1)S(1)} %update.4.refs_0_, bf16[512,256]{1,0:T(8,128)(2,1)S(1)} %collective-permute-done.30.refs_1_, ...), custom_call_target="tpu_custom_call" | custom-call | flops 4294967296 | bytes 16777216 | tf_op jit(solution)/shard_map/terms/pallas_call | solution.py:251
  230.5 1.0 collective-permute-start.37
  231.5 2.0 collective-permute-start.38
  233.5 11.5 %terms.10 = (bf16[512,256]{1,0:T(8,128)(2,1)S(1)}, f32[512,256]{1,0:T(8,128)S(1)}) custom-call(s32[2]{0:T(128)S(1)} %pad_add_fusion.place_ref, bf16[2048,4096]{1,0:T(8,128)(2,1)} %copy-done, bf16[2048,4096]{1,0:T(8,128)(2,1)} %copy-done.1, bf16[512,256]{1,0:T(8,128)(2,1)S(1)} %update.4.refs_0_, bf16[512,256]{1,0:T(8,128)(2,1)S(1)} %collective-permute-done.30.refs_1_, ...), custom_call_target="tpu_custom_call" | custom-call | flops 4294967296 | bytes 16777216 | tf_op jit(solution)/shard_map/terms/pallas_call | solution.py:251
  245.6 5.6 %collective-permute-done.37.refs_0_ = bf16[512,256]{1,0:T(8,128)(2,1)S(1)} collective-permute-done((bf16[512,256]{1,0:T(8,128)(2,1)S(1)}, bf16[512,256]{1,0:T(8,128)(2,1)S(1)}, u32[]{:S(2)}, u32[]{:S(2)}) %collective-permute-start.37) | collective-permute-done | bytes 262176 | tf_op jit(solution)/shard_map/ppermute | solution.py:319
  251.3 5.4 %collective-permute-done.39.refs_2_ = bf16[512,256]{1,0:T(8,128)(2,1)S(1)} collective-permute-done((bf16[512,256]{1,0:T(8,128)(2,1)S(1)}, bf16[512,256]{1,0:T(8,128)(2,1)S(1)}, u32[]{:S(2)}, u32[]{:S(2)}) %collective-permute-start.39) | collective-permute-done | bytes 262176 | tf_op jit(solution)/shard_map/ppermute | solution.py:319
  256.7 2.1 update.5
  (59 shorter events, 10.2 us)
Async XLA Ops:
  0.7 0.9 copy-start.2
  1.6 38.7 %copy-start.4 = (s32[2048]{0:T(1024)S(1)}, s32[2048]{0:T(1024)}, u32[]{:S(2)}) copy-start(s32[2048]{0:T(1024)} %param.6) | copy-start | bytes 24580
  32.7 4.9 %collective-permute-start = (bf16[128,128]{1,0:T(8,128)(2,1)S(1)}, bf16[128,128]{1,0:T(8,128)(2,1)S(1)}, u32[]{:S(2)}, u32[]{:S(2)}) collective-permute-start(bf16[128,128]{1,0:T(8,128)(2,1)S(1)} %bitcast.17), channel_id=1, source_target_pairs={{0,4},{4,0},{8,12},{12,8},{16,20},{20,16},{24,28},{28,24},{1,5},{5... | collective-permute-start | bytes 98312 | tf_op jit(solution)/shard_map/ppermute | solution.py:319
  33.2 7.0 %collective-permute-start.1 = (bf16[128,128]{1,0:T(8,128)(2,1)S(1)}, bf16[128,128]{1,0:T(8,128)(2,1)S(1)}, u32[]{:S(2)}, u32[]{:S(2)}) collective-permute-start(bf16[128,128]{1,0:T(8,128)(2,1)S(1)} %bitcast.16), channel_id=1, source_target_pairs={{0,8},{4,12},{8,0},{12,4},{16,24},{20,28},{24,16},{28,20},{1,9},{5... | collective-permute-start | bytes 98312 | tf_op jit(solution)/shard_map/ppermute | solution.py:319
  35.8 4.6 %collective-permute-start.2 = (bf16[128,128]{1,0:T(8,128)(2,1)S(1)}, bf16[128,128]{1,0:T(8,128)(2,1)S(1)}, u32[]{:S(2)}, u32[]{:S(2)}) collective-permute-start(bf16[128,128]{1,0:T(8,128)(2,1)S(1)} %bitcast.15), channel_id=1, source_target_pairs={{0,12},{4,8},{8,4},{12,0},{16,28},{20,24},{24,20},{28,16},{1,13},{... | collective-permute-start | bytes 98312 | tf_op jit(solution)/shard_map/ppermute | solution.py:319
  35.8 4.6 %collective-permute-start.3 = (bf16[128,128]{1,0:T(8,128)(2,1)S(1)}, bf16[128,128]{1,0:T(8,128)(2,1)S(1)}, u32[]{:S(2)}, u32[]{:S(2)}) collective-permute-start(bf16[128,128]{1,0:T(8,128)(2,1)S(1)} %bitcast.14), channel_id=1, source_target_pairs={{0,16},{4,20},{8,24},{12,28},{16,0},{20,4},{24,8},{28,12},{1,17},{... | collective-permute-start | bytes 98312 | tf_op jit(solution)/shard_map/ppermute | solution.py:319
  37.6 3.5 %collective-permute-start.4 = (bf16[128,128]{1,0:T(8,128)(2,1)S(1)}, bf16[128,128]{1,0:T(8,128)(2,1)S(1)}, u32[]{:S(2)}, u32[]{:S(2)}) collective-permute-start(bf16[128,128]{1,0:T(8,128)(2,1)S(1)} %bitcast.13), channel_id=1, source_target_pairs={{0,20},{4,16},{8,28},{12,24},{16,4},{20,0},{24,12},{28,8},{1,21},{... | collective-permute-start | bytes 98312 | tf_op jit(solution)/shard_map/ppermute | solution.py:319
  37.6 4.8 %collective-permute-start.5 = (bf16[128,128]{1,0:T(8,128)(2,1)S(1)}, bf16[128,128]{1,0:T(8,128)(2,1)S(1)}, u32[]{:S(2)}, u32[]{:S(2)}) collective-permute-start(bf16[128,128]{1,0:T(8,128)(2,1)S(1)} %bitcast.12), channel_id=1, source_target_pairs={{0,24},{4,28},{8,16},{12,20},{16,8},{20,12},{24,0},{28,4},{1,25},{... | collective-permute-start | bytes 98312 | tf_op jit(solution)/shard_map/ppermute | solution.py:319
  40.2 4.2 %collective-permute-start.6 = (bf16[128,128]{1,0:T(8,128)(2,1)S(1)}, bf16[128,128]{1,0:T(8,128)(2,1)S(1)}, u32[]{:S(2)}, u32[]{:S(2)}) collective-permute-start(bf16[128,128]{1,0:T(8,128)(2,1)S(1)} %bitcast.11), channel_id=1, source_target_pairs={{0,28},{4,24},{8,20},{12,16},{16,12},{20,8},{24,4},{28,0},{1,29},{... | collective-permute-start | bytes 98312 | tf_op jit(solution)/shard_map/ppermute | solution.py:319
  47.6 4.5 %collective-permute-start.7 = (bf16[256,128]{1,0:T(8,128)(2,1)S(1)}, bf16[256,128]{1,0:T(8,128)(2,1)S(1)}, u32[]{:S(2)}, u32[]{:S(2)}) collective-permute-start(bf16[256,128]{1,0:T(8,128)(2,1)S(1)} %get-tuple-element.35), channel_id=1, source_target_pairs={{0,1},{1,0},{2,3},{3,2},{4,5},{5,4},{6,7},{7,6},{8,9},{9,8},{10,11... | collective-permute-start | bytes 196616 | tf_op jit(solution)/shard_map/ppermute | solution.py:319
  49.3 7.6 %collective-permute-start.8 = (bf16[256,128]{1,0:T(8,128)(2,1)S(1)}, bf16[256,128]{1,0:T(8,128)(2,1)S(1)}, u32[]{:S(2)}, u32[]{:S(2)}) collective-permute-start(bf16[256,128]{1,0:T(8,128)(2,1)S(1)} %get-tuple-element.36), channel_id=1, source_target_pairs={{0,2},{1,3},{2,0},{3,1},{4,6},{5,7},{6,4},{7,5},{8,10},{9,11},{10,... | collective-permute-start | bytes 196616 | tf_op jit(solution)/shard_map/ppermute | solution.py:319
  51.8 6.2 %collective-permute-start.9 = (bf16[256,128]{1,0:T(8,128)(2,1)S(1)}, bf16[256,128]{1,0:T(8,128)(2,1)S(1)}, u32[]{:S(2)}, u32[]{:S(2)}) collective-permute-start(bf16[256,128]{1,0:T(8,128)(2,1)S(1)} %get-tuple-element.37), channel_id=1, source_target_pairs={{0,3},{1,2},{2,1},{3,0},{4,7},{5,6},{6,5},{7,4},{8,11},{9,10},{10,... | collective-permute-start | bytes 196616 | tf_op jit(solution)/shard_map/ppermute | solution.py:319
  59.0 9.3 %collective-permute-start.11 = (bf16[512,256]{1,0:T(8,128)(2,1)S(1)}, bf16[512,256]{1,0:T(8,128)(2,1)S(1)}, u32[]{:S(2)}, u32[]{:S(2)}) collective-permute-start(bf16[512,256]{1,0:T(8,128)(2,1)S(1)} %panel.1.refs_0_.refs_3_), channel_id=1, source_target_pairs={{0,8},{4,12},{8,0},{12,4},{16,24},{20,28},{24,16},{28,20},{1,9},{5... | collective-permute-start | bytes 786440 | tf_op jit(solution)/shard_map/ppermute | solution.py:319
  59.6 12.0 %collective-permute-start.13 = (bf16[512,256]{1,0:T(8,128)(2,1)S(1)}, bf16[512,256]{1,0:T(8,128)(2,1)S(1)}, u32[]{:S(2)}, u32[]{:S(2)}) collective-permute-start(bf16[512,256]{1,0:T(8,128)(2,1)S(1)} %panel.1.refs_0_.refs_3_), channel_id=1, source_target_pairs={{0,16},{4,20},{8,24},{12,28},{16,0},{20,4},{24,8},{28,12},{1,17},{... | collective-permute-start | bytes 786440 | tf_op jit(solution)/shard_map/ppermute | solution.py:319
  60.7 10.9 %collective-permute-start.15 = (bf16[512,256]{1,0:T(8,128)(2,1)S(1)}, bf16[512,256]{1,0:T(8,128)(2,1)S(1)}, u32[]{:S(2)}, u32[]{:S(2)}) collective-permute-start(bf16[512,256]{1,0:T(8,128)(2,1)S(1)} %panel.1.refs_0_.refs_3_), channel_id=1, source_target_pairs={{0,24},{4,28},{8,16},{12,20},{16,8},{20,12},{24,0},{28,4},{1,25},{... | collective-permute-start | bytes 786440 | tf_op jit(solution)/shard_map/ppermute | solution.py:319
  62.6 47.2 %collective-permute-start.10 = (bf16[512,256]{1,0:T(8,128)(2,1)S(1)}, bf16[512,256]{1,0:T(8,128)(2,1)S(1)}, u32[]{:S(2)}, u32[]{:S(2)}) collective-permute-start(bf16[512,256]{1,0:T(8,128)(2,1)S(1)} %panel.1.refs_0_.refs_3_), channel_id=1, source_target_pairs={{0,4},{4,0},{8,12},{12,8},{16,20},{20,16},{24,28},{28,24},{1,5},{5... | collective-permute-start | bytes 786440 | tf_op jit(solution)/shard_map/ppermute | solution.py:319
  68.3 41.5 %collective-permute-start.12 = (bf16[512,256]{1,0:T(8,128)(2,1)S(1)}, bf16[512,256]{1,0:T(8,128)(2,1)S(1)}, u32[]{:S(2)}, u32[]{:S(2)}) collective-permute-start(bf16[512,256]{1,0:T(8,128)(2,1)S(1)} %collective-permute-done.11.refs_2_), channel_id=1, source_target_pairs={{0,4},{4,0},{8,12},{12,8},{16,20},{20,16},{24,28},{28,24},{1,5},{5... | collective-permute-start | bytes 786440 | tf_op jit(solution)/shard_map/ppermute | solution.py:319
  71.6 38.2 %collective-permute-start.14 = (bf16[512,256]{1,0:T(8,128)(2,1)S(1)}, bf16[512,256]{1,0:T(8,128)(2,1)S(1)}, u32[]{:S(2)}, u32[]{:S(2)}) collective-permute-start(bf16[512,256]{1,0:T(8,128)(2,1)S(1)} %collective-permute-done.13.refs_4_), channel_id=1, source_target_pairs={{0,4},{4,0},{8,12},{12,8},{16,20},{20,16},{24,28},{28,24},{1,5},{5... | collective-permute-start | bytes 786440 | tf_op jit(solution)/shard_map/ppermute | solution.py:319
  71.6 38.2 %collective-permute-start.16 = (bf16[512,256]{1,0:T(8,128)(2,1)S(1)}, bf16[512,256]{1,0:T(8,128)(2,1)S(1)}, u32[]{:S(2)}, u32[]{:S(2)}) collective-permute-start(bf16[512,256]{1,0:T(8,128)(2,1)S(1)} %collective-permute-done.15.refs_6_), channel_id=1, source_target_pairs={{0,4},{4,0},{8,12},{12,8},{16,20},{20,16},{24,28},{28,24},{1,5},{5... | collective-permute-start | bytes 786440 | tf_op jit(solution)/shard_map/ppermute | solution.py:319
  85.2 5.8 %copy-start = (bf16[2048,4096]{1,0:T(8,128)(2,1)}, bf16[2048,4096]{1,0:T(8,128)(2,1)S(1)}, u32[]{:S(2)}) copy-start(bf16[2048,4096]{1,0:T(8,128)(2,1)S(1)} %relay.2.real_ref) | copy-start | bytes 50331652
  104.0 5.8 %copy-start.1 = (bf16[2048,4096]{1,0:T(8,128)(2,1)}, bf16[2048,4096]{1,0:T(8,128)(2,1)S(1)}, u32[]{:S(2)}) copy-start(bf16[2048,4096]{1,0:T(8,128)(2,1)S(1)} %relay.3.imag_ref) | copy-start | bytes 50331652
  109.8 37.6 %copy-start.3 = (f32[2]{0:T(128)S(1)}, f32[2]{0:T(128)}, u32[]{:S(2)}) copy-start(f32[2]{0:T(128)} %wave_ref.5) | copy-start | bytes 28
  121.3 21.2 %collective-permute-start.17 = (bf16[512,256]{1,0:T(8,128)(2,1)S(1)}, bf16[512,256]{1,0:T(8,128)(2,1)S(1)}, u32[]{:S(2)}, u32[]{:S(2)}) collective-permute-start(bf16[512,256]{1,0:T(8,128)(2,1)S(1)} %get-tuple-element.39), channel_id=1, source_target_pairs={{0,2},{1,3},{2,0},{3,1},{4,6},{5,7},{6,4},{7,5},{8,10},{9,11},{10,... | collective-permute-start | bytes 786440 | tf_op jit(solution)/shard_map/ppermute | solution.py:319
  123.5 19.1 %collective-permute-start.18 = (bf16[512,256]{1,0:T(8,128)(2,1)S(1)}, bf16[512,256]{1,0:T(8,128)(2,1)S(1)}, u32[]{:S(2)}, u32[]{:S(2)}) collective-permute-start(bf16[512,256]{1,0:T(8,128)(2,1)S(1)} %get-tuple-element.40), channel_id=1, source_target_pairs={{0,3},{1,2},{2,1},{3,0},{4,7},{5,6},{6,5},{7,4},{8,11},{9,10},{10,... | collective-permute-start | bytes 786440 | tf_op jit(solution)/shard_map/ppermute | solution.py:319
  136.4 10.9 %collective-permute-start.19 = (bf16[512,256]{1,0:T(8,128)(2,1)S(1)}, bf16[512,256]{1,0:T(8,128)(2,1)S(1)}, u32[]{:S(2)}, u32[]{:S(2)}) collective-permute-start(bf16[512,256]{1,0:T(8,128)(2,1)S(1)} %get-tuple-element.41), channel_id=1, source_target_pairs={{0,1},{1,0},{2,3},{3,2},{4,5},{5,4},{6,7},{7,6},{8,9},{9,8},{10,11... | collective-permute-start | bytes 786440 | tf_op jit(solution)/shard_map/ppermute | solution.py:319
  148.1 9.2 %collective-permute-start.21 = (bf16[512,256]{1,0:T(8,128)(2,1)S(1)}, bf16[512,256]{1,0:T(8,128)(2,1)S(1)}, u32[]{:S(2)}, u32[]{:S(2)}) collective-permute-start(bf16[512,256]{1,0:T(8,128)(2,1)S(1)} %update.3.refs_0_), channel_id=1, source_target_pairs={{0,8},{4,12},{8,0},{12,4},{16,24},{20,28},{24,16},{28,20},{1,9},{5... | collective-permute-start | bytes 786440 | tf_op jit(solution)/shard_map/ppermute | solution.py:319
  149.6 13.6 %collective-permute-start.23 = (bf16[512,256]{1,0:T(8,128)(2,1)S(1)}, bf16[512,256]{1,0:T(8,128)(2,1)S(1)}, u32[]{:S(2)}, u32[]{:S(2)}) collective-permute-start(bf16[512,256]{1,0:T(8,128)(2,1)S(1)} %update.3.refs_0_), channel_id=1, source_target_pairs={{0,16},{4,20},{8,24},{12,28},{16,0},{20,4},{24,8},{28,12},{1,17},{... | collective-permute-start | bytes 786440 | tf_op jit(solution)/shard_map/ppermute | solution.py:319
  150.2 13.1 %collective-permute-start.25 = (bf16[512,256]{1,0:T(8,128)(2,1)S(1)}, bf16[512,256]{1,0:T(8,128)(2,1)S(1)}, u32[]{:S(2)}, u32[]{:S(2)}) collective-permute-start(bf16[512,256]{1,0:T(8,128)(2,1)S(1)} %update.3.refs_0_), channel_id=1, source_target_pairs={{0,24},{4,28},{8,16},{12,20},{16,8},{20,12},{24,0},{28,4},{1,25},{... | collective-permute-start | bytes 786440 | tf_op jit(solution)/shard_map/ppermute | solution.py:319
  151.6 12.1 %collective-permute-start.20 = (bf16[512,256]{1,0:T(8,128)(2,1)S(1)}, bf16[512,256]{1,0:T(8,128)(2,1)S(1)}, u32[]{:S(2)}, u32[]{:S(2)}) collective-permute-start(bf16[512,256]{1,0:T(8,128)(2,1)S(1)} %update.3.refs_0_), channel_id=1, source_target_pairs={{0,4},{4,0},{8,12},{12,8},{16,20},{20,16},{24,28},{28,24},{1,5},{5... | collective-permute-start | bytes 786440 | tf_op jit(solution)/shard_map/ppermute | solution.py:319
  157.3 6.4 %collective-permute-start.22 = (bf16[512,256]{1,0:T(8,128)(2,1)S(1)}, bf16[512,256]{1,0:T(8,128)(2,1)S(1)}, u32[]{:S(2)}, u32[]{:S(2)}) collective-permute-start(bf16[512,256]{1,0:T(8,128)(2,1)S(1)} %collective-permute-done.21.refs_2_), channel_id=1, source_target_pairs={{0,4},{4,0},{8,12},{12,8},{16,20},{20,16},{24,28},{28,24},{1,5},{5... | collective-permute-start | bytes 786440 | tf_op jit(solution)/shard_map/ppermute | solution.py:319
  163.2 1.5 collective-permute-start.24
  163.2 1.9 collective-permute-start.26
  176.6 20.1 %collective-permute-start.27 = (bf16[512,256]{1,0:T(8,128)(2,1)S(1)}, bf16[512,256]{1,0:T(8,128)(2,1)S(1)}, u32[]{:S(2)}, u32[]{:S(2)}) collective-permute-start(bf16[512,256]{1,0:T(8,128)(2,1)S(1)} %get-tuple-element.43), channel_id=1, source_target_pairs={{0,2},{1,3},{2,0},{3,1},{4,6},{5,7},{6,4},{7,5},{8,10},{9,11},{10,... | collective-permute-start | bytes 786440 | tf_op jit(solution)/shard_map/ppermute | solution.py:319
  176.7 20.0 %collective-permute-start.28 = (bf16[512,256]{1,0:T(8,128)(2,1)S(1)}, bf16[512,256]{1,0:T(8,128)(2,1)S(1)}, u32[]{:S(2)}, u32[]{:S(2)}) collective-permute-start(bf16[512,256]{1,0:T(8,128)(2,1)S(1)} %get-tuple-element.44), channel_id=1, source_target_pairs={{0,3},{1,2},{2,1},{3,0},{4,7},{5,6},{6,5},{7,4},{8,11},{9,10},{10,... | collective-permute-start | bytes 786440 | tf_op jit(solution)/shard_map/ppermute | solution.py:319
  190.7 11.5 %collective-permute-start.29 = (bf16[512,256]{1,0:T(8,128)(2,1)S(1)}, bf16[512,256]{1,0:T(8,128)(2,1)S(1)}, u32[]{:S(2)}, u32[]{:S(2)}) collective-permute-start(bf16[512,256]{1,0:T(8,128)(2,1)S(1)} %get-tuple-element.45), channel_id=1, source_target_pairs={{0,1},{1,0},{2,3},{3,2},{4,5},{5,4},{6,7},{7,6},{8,9},{9,8},{10,11... | collective-permute-start | bytes 786440 | tf_op jit(solution)/shard_map/ppermute | solution.py:319
  202.9 9.2 %collective-permute-start.31 = (bf16[512,256]{1,0:T(8,128)(2,1)S(1)}, bf16[512,256]{1,0:T(8,128)(2,1)S(1)}, u32[]{:S(2)}, u32[]{:S(2)}) collective-permute-start(bf16[512,256]{1,0:T(8,128)(2,1)S(1)} %update.4.refs_0_), channel_id=1, source_target_pairs={{0,8},{4,12},{8,0},{12,4},{16,24},{20,28},{24,16},{28,20},{1,9},{5... | collective-permute-start | bytes 786440 | tf_op jit(solution)/shard_map/ppermute | solution.py:319
  203.5 13.6 %collective-permute-start.33 = (bf16[512,256]{1,0:T(8,128)(2,1)S(1)}, bf16[512,256]{1,0:T(8,128)(2,1)S(1)}, u32[]{:S(2)}, u32[]{:S(2)}) collective-permute-start(bf16[512,256]{1,0:T(8,128)(2,1)S(1)} %update.4.refs_0_), channel_id=1, source_target_pairs={{0,16},{4,20},{8,24},{12,28},{16,0},{20,4},{24,8},{28,12},{1,17},{... | collective-permute-start | bytes 786440 | tf_op jit(solution)/shard_map/ppermute | solution.py:319
  205.0 12.1 %collective-permute-start.35 = (bf16[512,256]{1,0:T(8,128)(2,1)S(1)}, bf16[512,256]{1,0:T(8,128)(2,1)S(1)}, u32[]{:S(2)}, u32[]{:S(2)}) collective-permute-start(bf16[512,256]{1,0:T(8,128)(2,1)S(1)} %update.4.refs_0_), channel_id=1, source_target_pairs={{0,24},{4,28},{8,16},{12,20},{16,8},{20,12},{24,0},{28,4},{1,25},{... | collective-permute-start | bytes 786440 | tf_op jit(solution)/shard_map/ppermute | solution.py:319
  206.5 11.1 %collective-permute-start.30 = (bf16[512,256]{1,0:T(8,128)(2,1)S(1)}, bf16[512,256]{1,0:T(8,128)(2,1)S(1)}, u32[]{:S(2)}, u32[]{:S(2)}) collective-permute-start(bf16[512,256]{1,0:T(8,128)(2,1)S(1)} %update.4.refs_0_), channel_id=1, source_target_pairs={{0,4},{4,0},{8,12},{12,8},{16,20},{20,16},{24,28},{28,24},{1,5},{5... | collective-permute-start | bytes 786440 | tf_op jit(solution)/shard_map/ppermute | solution.py:319
  212.2 5.5 %collective-permute-start.32 = (bf16[512,256]{1,0:T(8,128)(2,1)S(1)}, bf16[512,256]{1,0:T(8,128)(2,1)S(1)}, u32[]{:S(2)}, u32[]{:S(2)}) collective-permute-start(bf16[512,256]{1,0:T(8,128)(2,1)S(1)} %collective-permute-done.31.refs_2_), channel_id=1, source_target_pairs={{0,4},{4,0},{8,12},{12,8},{16,20},{20,16},{24,28},{28,24},{1,5},{5... | collective-permute-start | bytes 786440 | tf_op jit(solution)/shard_map/ppermute | solution.py:319
  217.1 1.5 collective-permute-start.34
  217.1 1.9 collective-permute-start.36
  230.5 20.8 %collective-permute-start.37 = (bf16[512,256]{1,0:T(8,128)(2,1)S(1)}, bf16[512,256]{1,0:T(8,128)(2,1)S(1)}, u32[]{:S(2)}, u32[]{:S(2)}) collective-permute-start(bf16[512,256]{1,0:T(8,128)(2,1)S(1)} %get-tuple-element.47), channel_id=1, source_target_pairs={{0,2},{1,3},{2,0},{3,1},{4,6},{5,7},{6,4},{7,5},{8,10},{9,11},{10,... | collective-permute-start | bytes 786440 | tf_op jit(solution)/shard_map/ppermute | solution.py:319
  231.5 19.7 %collective-permute-start.38 = (bf16[512,256]{1,0:T(8,128)(2,1)S(1)}, bf16[512,256]{1,0:T(8,128)(2,1)S(1)}, u32[]{:S(2)}, u32[]{:S(2)}) collective-permute-start(bf16[512,256]{1,0:T(8,128)(2,1)S(1)} %get-tuple-element.48), channel_id=1, source_target_pairs={{0,3},{1,2},{2,1},{3,0},{4,7},{5,6},{6,5},{7,4},{8,11},{9,10},{10,... | collective-permute-start | bytes 786440 | tf_op jit(solution)/shard_map/ppermute | solution.py:319
  245.0 11.6 %collective-permute-start.39 = (bf16[512,256]{1,0:T(8,128)(2,1)S(1)}, bf16[512,256]{1,0:T(8,128)(2,1)S(1)}, u32[]{:S(2)}, u32[]{:S(2)}) collective-permute-start(bf16[512,256]{1,0:T(8,128)(2,1)S(1)} %get-tuple-element.49), channel_id=1, source_target_pairs={{0,1},{1,0},{2,3},{3,2},{4,5},{5,4},{6,7},{7,6},{8,9},{9,8},{10,11... | collective-permute-start | bytes 786440 | tf_op jit(solution)/shard_map/ppermute | solution.py:319
